TPU v7x, 32 devices: a whole 2x2x4 slice. The times are simulated.
32 devices in a mesh: chan: 8 (over y, x, core), win: 4 (over z).
Axes of the slice: x: 2, y: 2, z: 4, core: 2. Of those that a mesh axis runs over, the one named last changes fastest.
Arguments:
- strain: bfloat16 [384, 4, 1024], P('chan', 'win'), may hold values from -384 to 384
- seg_ids: int32 [384], replicated, may hold values from 0 to 31, never falling along the last dimension, each value on 1 to 24 neighbouring positions
- dead: int32 [32], replicated, may hold values 0 or 1
- radius: int32 [384], P('chan'), may hold values from 1 to 8, as said below
Outputs:
- cross_spectra: bfloat16 [4, 2, 384, 384], P('win', None, 'chan')
Inputs may be any that keep to these rules, and one draw needn't show every extreme that they name: `seg_ids`: segment numbers never fall along the fiber; a change of segment between neighbouring channels marks a splice. Every segment has 1 to 24 channels, and one has exactly that many. Some channel has radius 8.
All inputs are finite; a program needn't handle non-finite values.
Results may differ from a plain program's by a relative error of at most 0.0023.
Values may be sent and summed in bfloat16 or wider, within the bound.
A program may use at most 64 MiB of HBM per device.

v0:
```python
import functools
import math

import jax
import jax.numpy as jnp
import numpy as np
from jax import lax
from jax.experimental import pallas as pl
from jax.experimental.pallas import tpu as pltpu
from jax.sharding import PartitionSpec as P

SAMPLES = 1024
FREQ_BINS = 128
FIRST_BIN = 8
SMOOTH_BINS = 4
MOST_REACH = 8
FLOOR_POWER = 0.01
LANES = 128
TABLE_CUTS = 2
GROUP = 8
PEAK = 3.0
TOP_CODE = 32767.0
ROOT_SCALE = math.log2(TOP_CODE) - math.log2(PEAK) / 8.0

MESH = pl.DeviceIdType.MESH
F32 = jnp.float32
BF16 = jnp.bfloat16


def fourier_table(bands):
    band_bins = FREQ_BINS // bands
    half = SAMPLES // 2
    t = np.arange(half, dtype=np.int64)
    bins = FIRST_BIN + np.arange(FREQ_BINS, dtype=np.int64)
    angles = np.pi / SAMPLES * ((2 * t[:, None] + 1) * bins[None, :] % (2 * SAMPLES))
    taper = 0.5 - 0.5 * np.cos(2.0 * np.pi / SAMPLES * (t + 0.5))
    weights = taper[:, None] / np.sqrt(float(SAMPLES))
    cos, sin = weights * np.cos(angles), -weights * np.sin(angles)
    both = np.stack(
        [cos.reshape(half, bands, band_bins), sin.reshape(half, bands, band_bins)], axis=2
    ).reshape(half, 2 * FREQ_BINS)
    return both.astype(np.float32).reshape(TABLE_CUTS, half // TABLE_CUTS, -1)


def split3(x):
    high = x.astype(BF16)
    rest = x - high.astype(F32)
    middle = rest.astype(BF16)
    low = (rest - middle.astype(F32)).astype(BF16)
    return high, middle, low


def column_of(row, length, shift=0):
    shape = (length, row.shape[1])
    hit = lax.broadcasted_iota(jnp.int32, shape, 1) == lax.broadcasted_iota(jnp.int32, shape, 0) + shift
    return jnp.sum(jnp.where(hit, row, 0), axis=1, keepdims=True)


def links(seg, dead, radius, me, rows):
    channels, segments = seg.shape[1], dead.shape[1]
    start = me * rows - MOST_REACH
    turned = pltpu.roll(jnp.broadcast_to(seg, (8, channels)), lax.rem(channels - start, channels), 1)
    near = turned[0:1, 0:LANES]
    lane = lax.broadcasted_iota(jnp.int32, (1, LANES), 1)
    inside = (lane + start >= 0) & (lane + start < channels)
    dead_column = column_of(dead, segments)
    is_segment = lax.broadcasted_iota(jnp.int32, (segments, LANES), 0) == near
    dead_near = jnp.sum(jnp.where(is_segment, dead_column, 0), axis=0, keepdims=True)
    alive_near = jnp.where(inside, 1 - dead_near, 0)
    own_segs = column_of(near, rows, MOST_REACH)
    alive_own = column_of(alive_near, rows, MOST_REACH).astype(F32)
    reach = column_of(radius, rows)
    shape = (rows, LANES)
    offsets = lax.broadcasted_iota(jnp.int32, shape, 1) - lax.broadcasted_iota(jnp.int32, shape, 0) - MOST_REACH
    linked = (jnp.abs(offsets) <= reach) & (near == own_segs) & (alive_near > 0)
    linked = jnp.where(linked, 1.0, 0.0)
    counts = jnp.maximum(jnp.sum(linked, axis=1, keepdims=True), 1.0)
    lane = lax.broadcasted_iota(jnp.int32, shape, 1)
    own_first = pltpu.roll(linked, LANES - MOST_REACH, 1)
    linked = jnp.where(lane < rows, own_first, jnp.where(lane < rows + MOST_REACH, pltpu.roll(linked, rows, 1), linked))
    return linked[:, : rows + 2 * MOST_REACH].astype(BF16), alive_own, 1.0 / counts


def bin_of(lanes, bands):
    half = FREQ_BINS // bands
    return lanes // (2 * half) * half + lanes % half


def smoothing(bands):
    lanes = 2 * FREQ_BINS
    bins = bin_of(lax.broadcasted_iota(jnp.int32, (1, lanes), 1), bands)
    apart = bin_of(lax.broadcasted_iota(jnp.int32, (lanes, 1), 0), bands) - bins
    nearby = jnp.where(jnp.abs(apart) <= SMOOTH_BINS, 1.0, 0.0).astype(BF16)
    members = jnp.minimum(bins + SMOOTH_BINS, FREQ_BINS - 1) - jnp.maximum(bins - SMOOTH_BINS, 0) + 1
    return nearby, 1.0 / members.astype(F32)


def dot(a, b):
    return jnp.dot(a, b, preferred_element_type=F32)


def dot_rows(a, b):
    return lax.dot_general(a, b, (((1,), (1,)), ((), ())), preferred_element_type=F32)


def quantized(x, power, mean_power):
    root = jnp.exp2((jnp.log2(power) - jnp.log2(mean_power)) * 0.0625 + ROOT_SCALE)
    code = jnp.minimum(root + 0.5, TOP_CODE).astype(jnp.int32)
    return jnp.where(x < 0, -code, code)


def restored(codes):
    y = codes.astype(jnp.int32).astype(F32) * (1.0 / TOP_CODE)
    y2 = y * y
    y4 = y2 * y2
    size = (y4 * y4) * PEAK
    return jnp.where(y < 0, -size, size)


def split2(x):
    high = x.astype(BF16)
    return high, (x - high.astype(F32)).astype(BF16)


def for_each_peer(chans, me, act, order=(6, 7, 4, 5, 2, 3, 1)):
    if chans == GROUP:
        bits = [lax.rem(me // 2**i, 2) for i in range(3)]
        for k in order:
            act(k, me + sum((1 - 2 * bits[i]) * 2**i for i in range(3) if k >> i & 1))
    else:

        def step(k, carry):
            act(k, lax.rem(me + k, chans))
            return carry

        lax.fori_loop(1, chans, step, 0)


def kernel(
    chans, wins, strain_hbm, seg_hbm, dead_hbm, radius_hbm, table_hbm, out_ref,
    strain, seg, dead, radius, table, edges, halo_rows, blocks, chunks, arrived, right, load_sem, table_sem,
    halo_send, halo_recv, win_send, win_recv, pair_send, pair_recv,
):
    rows = strain_hbm.shape[0]
    width = 2 * FREQ_BINS
    me, win = lax.axis_index("chan"), lax.axis_index("win")

    strain_load = pltpu.make_async_copy(strain_hbm, strain, load_sem.at[0])
    table_loads = [
        pltpu.make_async_copy(table_hbm.at[i], table.at[i], table_sem.at[i]) for i in range(TABLE_CUTS)
    ]
    for load in [strain_load] + table_loads:
        load.start()

    barrier = pltpu.get_barrier_semaphore()

    def greet(k, peer):
        pl.semaphore_signal(barrier, inc=1, device_id={"chan": peer}, device_id_type=MESH)

    for_each_peer(chans, me, greet)
    for r in range(1, wins):
        pl.semaphore_signal(barrier, inc=1, device_id={"win": lax.rem(win + r, wins)}, device_id_type=MESH)

    loads = [
        pltpu.make_async_copy(src, dst, load_sem.at[1 + i])
        for i, (src, dst) in enumerate([(seg_hbm, seg), (dead_hbm, dead), (radius_hbm, radius)])
    ]
    for load in loads:
        load.start()

    nearby, per_member = smoothing(wins)
    for load in loads:
        load.wait()
    linked, alive, per_count = links(seg[...].reshape(1, -1), dead[...], radius[...], me, rows)

    strain_load.wait()
    cut = SAMPLES // 2 // TABLE_CUTS
    shape = (cut, cut)
    flips = lax.broadcasted_iota(jnp.int32, shape, 0) + lax.broadcasted_iota(jnp.int32, shape, 1) == cut - 1
    last_cuts = [strain[:, SAMPLES - (i + 1) * cut : SAMPLES - i * cut] for i in range(TABLE_CUTS)]
    backwards = dot(jnp.concatenate(last_cuts, axis=0), jnp.where(flips, 1.0, 0.0).astype(BF16)).astype(BF16)
    total = None
    for i in range(TABLE_CUTS):
        samples = jnp.concatenate(
            [strain[:, i * cut : (i + 1) * cut], backwards[i * rows : (i + 1) * rows]], axis=0
        )
        table_loads[i].wait()
        term = dot(samples, jnp.concatenate(split3(table[i]), axis=1))
        total = term if total is None else total + term
    total = total[:, :width] + total[:, width : 2 * width] + total[:, 2 * width :]
    is_cos = lax.broadcasted_iota(jnp.int32, (1, width), 1) % (width // wins) < width // wins // 2
    own = total[:rows] + jnp.where(is_cos, 1.0, -1.0) * total[rows:]
    edges[0] = own[rows - MOST_REACH :]
    edges[1] = own[:MOST_REACH]

    pl.semaphore_wait(barrier, chans - 1 + wins - 1)

    halos = [
        pltpu.make_async_remote_copy(
            src_ref=edges.at[side],
            dst_ref=halo_rows.at[side],
            send_sem=halo_send.at[side],
            recv_sem=halo_recv.at[side],
            device_id={"chan": lax.rem(me + step, chans)},
            device_id_type=MESH,
        )
        for side, step in enumerate((1, chans - 1))
    ]
    for halo in halos:
        halo.start()
    own_sums = dot(linked[:, :rows], jnp.concatenate(split3(own), axis=1))
    own_sums = own_sums[:, :width] + own_sums[:, width : 2 * width] + own_sums[:, 2 * width :]
    for halo in halos:
        halo.wait_recv()

    near_rows = halo_rows[...].reshape(2 * MOST_REACH, width)
    near_parts = jnp.concatenate(split3(near_rows), axis=1)
    sums = dot(linked[:, rows:], near_parts)
    sums = own_sums + (sums[:, :width] + sums[:, width : 2 * width] + sums[:, 2 * width :])
    spectra = alive * (own - sums * per_count)
    power = spectra * spectra
    smooth = dot(jnp.concatenate(split2(power), axis=0), nearby)
    smooth = (smooth[:rows] + smooth[rows:]) * per_member
    codes = quantized(spectra, power, jnp.maximum(smooth, FLOOR_POWER))

    for j in range(wins // 2):
        tile = codes[:, j * LANES : (j + 1) * LANES]
        turned = pltpu.roll(tile, LANES // 2, 1).astype(jnp.int16)
        tile = tile.astype(jnp.int16)
        for h in range(2):
            chunks[h, 2 * j + h] = tile
            chunks[h, 2 * j + 1 - h] = turned

    to_band = {}
    for r in range(wins - 1, 0, -1):
        band = win + sum((1 - 2 * lax.rem(win // 2**i, 2)) * 2**i for i in range(2) if r >> i & 1)
        copy = pltpu.make_async_remote_copy(
            src_ref=chunks.at[r % 2, band],
            dst_ref=arrived.at[r],
            send_sem=win_send.at[r],
            recv_sem=win_recv.at[r],
            device_id={"win": band},
            device_id_type=MESH,
        )
        copy.start()
        to_band[r] = copy

    def piece(owner, peer, pair):
        return pltpu.make_async_remote_copy(
            src_ref=blocks.at[pair, owner],
            dst_ref=blocks.at[pair, owner],
            send_sem=pair_send.at[pair],
            recv_sem=pair_recv.at[pair, owner],
            device_id={"chan": peer},
            device_id_type=MESH,
        )

    in_first = lax.broadcasted_iota(jnp.int32, (rows, LANES), 1) < LANES // 2
    is_re = lax.broadcasted_iota(jnp.int32, (rows, LANES), 1) % (LANES // 2) < LANES // 4
    pairs = wins // 2
    left = []
    for pair in range(pairs):
        if pair > 0:
            to_band[2 * pair].wait_recv()
        to_band[2 * pair + 1].wait_recv()
        even = chunks[0, win] if pair == 0 else arrived[2 * pair]
        both = jnp.where(in_first, even.astype(jnp.int32), arrived[2 * pair + 1].astype(jnp.int32))
        blocks[pair, me] = both.astype(jnp.int16)
        for_each_peer(chans, me, lambda k, peer: piece(me, peer, pair).start())
        x = restored(both)
        right[pair, me] = jnp.concatenate(split2(x), axis=1)
        after = pltpu.roll(x, LANES - LANES // 4, 1)
        before = pltpu.roll(x, LANES // 4, 1)
        high, low = split2(jnp.concatenate([x, jnp.where(is_re, after, -before)], axis=0))
        left.append(
            jnp.concatenate(
                [
                    jnp.concatenate([high, high], axis=1),
                    jnp.concatenate([low, jnp.zeros_like(low)], axis=1),
                ],
                axis=0,
            )
        )

    scale = 1.0 / FREQ_BINS

    def term(pair, g):
        return dot_rows(left[pair], right[pair, pl.ds(g * GROUP, GROUP)].reshape(GROUP * rows, 2 * LANES))

    def finished(acc):
        return ((acc[: 2 * rows] + acc[2 * rows :]) * scale).astype(out_ref.dtype)

    def take(pair, k, peer):
        piece(peer, peer, pair).wait_recv()
        right[pair, peer] = jnp.concatenate(split2(restored(blocks[pair, peer])), axis=1)

    def take_pair(pair):
        for_each_peer(chans, me, functools.partial(take, pair), (1, 2, 3, 4, 5, 6, 7))

    if chans == GROUP:
        acc = None
        for pair in range(pairs):
            take_pair(pair)
            acc = term(pair, 0) if acc is None else acc + term(pair, 0)
        out = finished(acc)
        out_ref[0, 0] = out[:rows]
        out_ref[0, 1] = out[rows:]
    else:
        for pair in range(pairs):
            take_pair(pair)

        @pl.loop(0, chans // GROUP)
        def _(g):
            out = finished(sum(term(pair, g) for pair in range(pairs)))
            at = pl.ds(pl.multiple_of(g * (GROUP * rows), LANES), GROUP * rows)
            out_ref[0, 0, :, at] = out[:rows]
            out_ref[0, 1, :, at] = out[rows:]

    for copy in halos + list(to_band.values()):
        copy.wait_send()
    for pair in range(pairs):
        sent = blocks.at[pair, pl.ds(0, chans - 1)]
        pltpu.make_async_remote_copy(
            src_ref=sent,
            dst_ref=sent,
            send_sem=pair_send.at[pair],
            recv_sem=pair_recv.at[pair, me],
            device_id={"chan": lax.rem(me + 1, chans)},
            device_id_type=MESH,
        ).wait_send()


def body(chans, wins, strain, seg_ids, dead, radius):
    rows, windows, samples = strain.shape
    table = jnp.asarray(fourier_table(wins))
    width = 2 * FREQ_BINS
    dma = pltpu.SemaphoreType.DMA
    hbm = pl.BlockSpec(memory_space=pltpu.HBM)
    i32, i16 = jnp.int32, jnp.int16
    return pl.pallas_call(
        functools.partial(kernel, chans, wins),
        out_shape=pltpu.VMEM((1, 2, rows, chans * rows), BF16),
        in_specs=[hbm] * 5,
        out_specs=pl.BlockSpec(memory_space=pltpu.VMEM),
        scratch_shapes=[
            pltpu.VMEM((rows, samples), BF16),
            pltpu.VMEM(seg_ids.shape, i32),
            pltpu.VMEM((1, dead.shape[0]), i32),
            pltpu.VMEM((1, rows), i32),
            pltpu.VMEM(table.shape, F32),
            pltpu.VMEM((2, MOST_REACH, width), F32),
            pltpu.VMEM((2, MOST_REACH, width), F32),
            pltpu.VMEM((wins // 2, chans, rows, LANES), i16),
            pltpu.VMEM((2, wins, rows, LANES), i16),
            pltpu.VMEM((wins, rows, LANES), i16),
            pltpu.VMEM((wins // 2, chans, rows, 2 * LANES), BF16),
            dma((4,)),
            dma((TABLE_CUTS,)),
            dma((2,)),
            dma((2,)),
            dma((wins,)),
            dma((wins,)),
            dma((wins // 2,)),
            dma((wins // 2, chans)),
        ],
        compiler_params=pltpu.CompilerParams(
            collective_id=0, has_side_effects=True, vmem_limit_bytes=(63 if chans == GROUP else 48) * 2**20
        ),
    )(
        strain.reshape(rows * windows, samples),
        seg_ids,
        dead.reshape(1, -1),
        radius.reshape(1, -1),
        table,
    )


def solution(mesh):
    return jax.shard_map(
        functools.partial(body, mesh.shape["chan"], mesh.shape["win"]),
        mesh=mesh,
        in_specs=(P("chan", "win", None), P(), P(), P("chan")),
        out_specs=P("win", None, "chan", None),
        check_vma=False,
    )
```

profile of v0, /device:TPU:0, one launch (start us, length us, event | category | flops | bytes accessed | tf_op | source)
XLA Modules:
  0.0 16.2 jit_solution(3532515497482369397)
XLA Ops:
  0.0 15.5 %shard_map.55 = bf16[1,2,48,384]{3,2,1,0:T(8,128)(2,1)S(1)} custom-call(bf16[48,1024]{1,0:T(8,128)(2,1)} %bitcast.3, s32[384]{0:T(512)} %seg_hbm.1, s32[1,32]{1,0:T(1,128)} %bitcast.4, s32[1,48]{1,0:T(1,128)} %bitcast.5, f32[2,256,256]{2,1,0:T(8,128)} %constant.2.clone.table_hbm), custom_call_target="tpu_custom_call" | custom-call | tf_op jit(solution)/shard_map/pallas_call | solution.py:340
  15.5 0.6 %copy.7 = bf16[1,2,48,384]{3,2,1,0:T(8,128)(2,1)} copy(bf16[1,2,48,384]{3,2,1,0:T(8,128)(2,1)S(1)} %shard_map.55) | data formatting | bytes 147456
where the time goes:
time: 16.3 us; the launch traced here: 16.2 us
  Pallas kernels  15.5 us (95%)
  local copies, waits for them, and re-layouts  0.64 us (4%)
    pallas_call x1, Pallas kernels, body(): pl.pallas_call(functools.partial(kernel, chans, wins), out_shape=pltpu.VM...  15.5 us
    unnamed x1, local copies, waits for them, and re-layouts  0.64 us

commit v1 on v0

--- a/solution.py
+++ b/solution.py
@@ -272,23 +272,16 @@
         after = pltpu.roll(x, LANES - LANES // 4, 1)
         before = pltpu.roll(x, LANES // 4, 1)
         high, low = split2(jnp.concatenate([x, jnp.where(is_re, after, -before)], axis=0))
-        left.append(
-            jnp.concatenate(
-                [
-                    jnp.concatenate([high, high], axis=1),
-                    jnp.concatenate([low, jnp.zeros_like(low)], axis=1),
-                ],
-                axis=0,
-            )
-        )
+        left.append(jnp.concatenate([high, high, low], axis=1))
 
     scale = 1.0 / FREQ_BINS
 
     def term(pair, g):
-        return dot_rows(left[pair], right[pair, pl.ds(g * GROUP, GROUP)].reshape(GROUP * rows, 2 * LANES))
+        parts = right[pair, pl.ds(g * GROUP, GROUP)].reshape(GROUP * rows, 2 * LANES)
+        return dot_rows(left[pair], jnp.concatenate([parts, parts[:, :LANES]], axis=1))
 
     def finished(acc):
-        return ((acc[: 2 * rows] + acc[2 * rows :]) * scale).astype(out_ref.dtype)
+        return (acc * scale).astype(out_ref.dtype)
 
     def take(pair, k, peer):
         piece(peer, peer, pair).wait_recv()

time: 16.3 us -> 16.4 us (level)
  no operation moved by 1% of the time
where the time goes in v1:
time: 16.4 us; the launch traced here: 16.2 us
  Pallas kernels  15.6 us (95%)
  local copies, waits for them, and re-layouts  0.64 us (4%)
    pallas_call x1, Pallas kernels, body(): pl.pallas_call(functools.partial(kernel, chans, wins), out_shape=pltpu.VM...  15.6 us
    unnamed x1, local copies, waits for them, and re-layouts  0.64 us

profile of v1, /device:TPU:0, one launch (start us, length us, event | category | flops | bytes accessed | tf_op | source)
XLA Modules:
  0.0 16.2 jit_solution(2202883986835009368)
XLA Ops:
  0.0 15.6 %shard_map.55 = bf16[1,2,48,384]{3,2,1,0:T(8,128)(2,1)S(1)} custom-call(bf16[48,1024]{1,0:T(8,128)(2,1)} %bitcast.3, s32[384]{0:T(512)} %seg_hbm.1, s32[1,32]{1,0:T(1,128)} %bitcast.4, s32[1,48]{1,0:T(1,128)} %bitcast.5, f32[2,256,256]{2,1,0:T(8,128)} %constant.2.clone.table_hbm), custom_call_target="tpu_custom_call" | custom-call | tf_op jit(solution)/shard_map/pallas_call | solution.py:333
  15.6 0.6 %copy.7 = bf16[1,2,48,384]{3,2,1,0:T(8,128)(2,1)} copy(bf16[1,2,48,384]{3,2,1,0:T(8,128)(2,1)S(1)} %shard_map.55) | data formatting | bytes 147456
